TPU v7x, 32 devices: a whole 2x2x4 slice. The times are simulated.
32 devices in a mesh: tp: 4 (over x, core), client: 4 (over z), region: 2 (over y).
Axes of the slice: x: 2, y: 2, z: 4, core: 2. Of those that a mesh axis runs over, the one named last changes fastest.
Arguments:
- hidden_in: bfloat16 [8, 2, 128, 1792], P(('client', 'region'), None, None, 'tp'), may hold values from -6 to 6
- target: bfloat16 [8, 2, 128, 1792], P(('client', 'region'), None, None, 'tp'), may hold values from -38 to 38, as said below
- up_weight: bfloat16 [1792, 7168], P(None, 'tp'), may hold values from -1 to 1
- down_weight: bfloat16 [7168, 1792], P('tp'), may hold values from -0.0625 to 0.0625
- noise_up: float32 [1792, 7168], P(('client', 'region'), 'tp'), may hold values from -6 to 6
- noise_down: float32 [7168, 1792], P('tp', ('client', 'region')), may hold values from -6 to 6
Outputs:
- new_up: float32 [1792, 7168], P(('client', 'region'), 'tp')
- new_down: float32 [7168, 1792], P('tp', ('client', 'region'))
Inputs may be any that keep to these rules, and one draw needn't show every extreme that they name: `target`: targets of every client and step.
All inputs are finite; a program needn't handle non-finite values.
Results may differ from a plain program's by a relative error of at most 0.014.
Values may be sent and summed in bfloat16 or wider, within the bound.
A program may use at most 128 MiB of HBM per device.

v0:
```python
import math

import jax
import jax.numpy as jnp
from jax import lax
from jax.sharding import PartitionSpec as P

D = 1792
F = 7168
STEPS = 2


local_rate = 0.5
clip_rms = 0.08
server_rate = 0.02


def gelu_back(pre, back):
    return jax.vjp(lambda value: jax.nn.gelu(value, approximate=True), pre)[1](back)[0]


def contract_rows(left, right):
    return lax.dot_general(
        left, right, (((0,), (0,)), ((), ())), preferred_element_type=jnp.float32
    )


def shards(hidden_in, target, up_weight, down_weight, noise_up, noise_down):
    inputs_all, goals_all = (
        lax.all_gather(hidden_in, "tp", axis=3, tiled=True),
        lax.all_gather(target, "tp", axis=3, tiled=True),
    )
    inputs_all = inputs_all[0]
    goals_all = goals_all[0]
    w_up, w_down = (up_weight, down_weight)
    acc_up = jnp.zeros(up_weight.shape, jnp.float32)
    acc_down = jnp.zeros(down_weight.shape, jnp.float32)
    for turn in range(STEPS):
        inputs = inputs_all[turn]
        xfloat = inputs.astype(jnp.float32)
        normed = (
            xfloat * lax.rsqrt(jnp.mean(xfloat * xfloat, axis=-1, keepdims=True) + 1e-06)
        ).astype(jnp.bfloat16)
        pre = jnp.dot(normed, w_up, preferred_element_type=jnp.float32)
        act = jax.nn.gelu(pre, approximate=True).astype(jnp.bfloat16)
        partial_out = jnp.dot(act, w_down, preferred_element_type=jnp.float32)
        output = xfloat + lax.psum(partial_out.astype(jnp.bfloat16), "tp").astype(jnp.float32)
        resid = ((output - goals_all[turn].astype(jnp.float32)) / inputs.shape[0]).astype(
            jnp.bfloat16
        )
        grad_down = contract_rows(act, resid)
        back = lax.dot_general(
            resid, w_down, (((1,), (1,)), ((), ())), preferred_element_type=jnp.float32
        )
        dpre = gelu_back(pre, back).astype(jnp.bfloat16)
        grad_up = contract_rows(normed, dpre)
        acc_up = acc_up + grad_up
        acc_down = acc_down + grad_down
        if turn + 1 < STEPS:
            w_up = (w_up.astype(jnp.float32) - local_rate * grad_up).astype(jnp.bfloat16)
            w_down = (w_down.astype(jnp.float32) - local_rate * grad_down).astype(jnp.bfloat16)
    delta_up = -local_rate * acc_up
    delta_down = -local_rate * acc_down
    squared = lax.psum(jnp.sum(delta_up * delta_up) + jnp.sum(delta_down * delta_down), "tp")
    bound = clip_rms * math.sqrt(2.0 * D * F)
    factor = bound / jnp.maximum(jnp.sqrt(squared), bound)
    clip_up = lax.optimization_barrier((delta_up * factor).astype(jnp.bfloat16)).astype(jnp.float32)
    clip_down = lax.optimization_barrier((delta_down * factor).astype(jnp.bfloat16)).astype(
        jnp.float32
    )
    summed_up, summed_down = (
        lax.psum_scatter(
            clip_up.astype(jnp.bfloat16), "client", scatter_dimension=0, tiled=True
        ).astype(jnp.float32),
        lax.psum_scatter(
            clip_down.astype(jnp.bfloat16), "client", scatter_dimension=1, tiled=True
        ).astype(jnp.float32),
    )
    client_count = lax.axis_size("client")
    region_count = lax.axis_size("region")
    count = client_count * region_count
    rows = D // count
    region_index = lax.axis_index("region")
    full_up, full_down = (
        lax.psum(summed_up.astype(jnp.bfloat16), "region").astype(jnp.float32),
        lax.psum(summed_down.astype(jnp.bfloat16), "region").astype(jnp.float32),
    )
    share_up = lax.dynamic_slice_in_dim(full_up, region_index * rows, rows, 0)
    share_down = lax.dynamic_slice_in_dim(full_down, region_index * rows, rows, 1)
    block = lax.axis_index("client") * region_count + region_index
    base_up = lax.dynamic_slice_in_dim(up_weight, block * rows, rows, 0).astype(jnp.float32)
    base_down = lax.dynamic_slice_in_dim(down_weight, block * rows, rows, 1).astype(jnp.float32)
    root = math.sqrt(count)
    scale = server_rate / (clip_rms * root)
    new_up = base_up + scale * (share_up + clip_rms * root * noise_up)
    new_down = base_down + scale * (share_down + clip_rms * root * noise_down)
    return (new_up, new_down)


def solution(mesh):
    placed = (
        P(("client", "region"), None, None, "tp"),
        P(("client", "region"), None, None, "tp"),
        P(None, "tp"),
        P("tp", None),
        P(("client", "region"), "tp"),
        P("tp", ("client", "region")),
    )
    return jax.shard_map(
        shards,
        mesh=mesh,
        in_specs=placed,
        out_specs=(P(("client", "region"), "tp"), P("tp", ("client", "region"))),
        check_vma=False,
    )
```

profile of v0, /device:TPU:25, one launch (start us, length us, event | category | flops | bytes accessed | tf_op | source)
XLA Modules:
  0.0 522.8 jit_solution(9554526460549865157)
XLA Ops:
  7.2 0.0 all-reduce.5.cloned.1.call-start
  7.2 1.2 copy.12
  8.4 9.8 %all_gather.6 = bf16[1,2,128,1792]{2,1,0,3:T(2,128)(2,1)S(1)} all-gather(bf16[1,2,128,448]{2,1,0,3:T(2,128)(2,1)S(1)} %copy.12), channel_id=1, replica_groups=mesh['tp'=4,'client'=4,'region'=2] {'tp'}, dimensions={3}, use_global_device_ids=true | all-gather | bytes 1146880 | tf_op jit(solution)/shard_map/all_gather | solution.py:30
  18.2 2.2 fusion.75
  20.4 2.3 copy.22
  22.8 0.2 fusion.16
  23.0 0.0 copy-start.12
  23.0 4.0 fusion.44
  27.0 0.9 copy-done.5
  28.0 1.9 convolution_convert_fusion.1
  29.9 0.0 all-reduce.5.cloned.1.call-update
  29.9 0.0 all-reduce.7.cloned.1.call-start
  30.0 0.2 copy.14
  30.2 10.8 %all_gather.7 = bf16[1,2,128,1792]{2,1,0,3:T(2,128)(2,1)S(1)} all-gather(bf16[1,2,128,448]{2,1,0,3:T(2,128)(2,1)S(1)} %copy.14), channel_id=1, replica_groups=mesh['tp'=4,'client'=4,'region'=2] {'tp'}, dimensions={3}, use_global_device_ids=true | all-gather | bytes 1146880 | tf_op jit(solution)/shard_map/all_gather | solution.py:31
  41.1 2.0 fusion.74
  43.1 2.3 copy.24
  45.5 0.2 fusion.21
  45.6 0.9 copy.23
  46.6 16.3 %all-reduce.5.cloned.1.call-done = bf16[128,1792]{1,0:T(8,128)(2,1)} async-done(((bf16[128,1792]{1,0:T(8,128)(2,1)}), bf16[128,1792]{1,0:T(8,128)(2,1)}) %all-reduce.5.cloned.1.call-update) | async-done | bytes 458768 | tf_op jit(solution)/shard_map/psum | solution.py:47
  63.0 11.8 %fusion.27 = f32[1792,1792]{1,0:T(8,128)} fusion(f32[128,1792]{1,0:T(8,128)} %copy-done.5, bf16[1,1,128,1792]{3,2,1,0:T(8,128)(2,1)S(1)} %copy.22, f32[128]{0:T(128)S(1)} %add_rsqrt_fusion.1, bf16[1792,1792]{1,0:T(8,128)(2,1)} %param.9, bf16[128,1792]{1,0:T(8,128)(2,1)} %all-reduce.5.cloned.1.call-done, bf16[1,1,128,1792]{3,2,1,0:T(8,128)(2,1)S(1)} %copy.23), kind=kOutput, calls=%fused_computation.50 | convolution fusion | flops 1651048448 | bytes 21561856 | tf_op jit(solution)/shard_map/dot_general | solution.py:23
  74.8 0.0 slice-start.3
  74.8 8.8 %fusion = f32[128,1792]{1,0:T(8,128)S(1)} fusion(f32[1792,1792]{1,0:T(8,128)} %fusion.27, bf16[1792,1792]{1,0:T(8,128)(2,1)} %param.8, bf16[1,1,128,1792]{3,2,1,0:T(8,128)(2,1)} %copy-done.1, f32[128]{0:T(128)S(1)} %add_rsqrt_fusion), kind=kOutput, calls=%fused_computation.8 | convolution fusion | flops 835616768 | bytes 20644352 | tf_op jit(solution)/shard_map/dot_general | solution.py:44
  83.7 2.1 fusion.66
  85.8 4.6 copy-done
  90.4 3.3 convolution_convert_fusion
  93.6 0.0 all-reduce.7.cloned.1.call-update
  93.6 0.3 reduce-scatter.7.cloned.1.call-start
  93.9 2.4 copy.25
  96.3 30.6 %all-reduce.7.cloned.1.call-done = bf16[128,1792]{1,0:T(8,128)(2,1)} async-done(((bf16[128,1792]{1,0:T(8,128)(2,1)}), bf16[128,1792]{1,0:T(8,128)(2,1)}) %all-reduce.7.cloned.1.call-update) | async-done | bytes 458768 | tf_op jit(solution)/shard_map/psum | solution.py:47
  126.9 19.4 %multiply_reduce_fusion.1 = (f32[]{:T(128)}, f32[1792,1792]{1,0:T(8,128)}) fusion(f32[1792,1792]{1,0:T(8,128)} %fusion.27, f32[128,1792]{1,0:T(8,128)S(1)} %fusion, bf16[128,1792]{1,0:T(8,128)(2,1)} %all-reduce.7.cloned.1.call-done, bf16[1,1,128,1792]{3,2,1,0:T(8,128)(2,1)S(1)} %copy.25, bf16[1,1,128,1792]{3,2,1,0:T(8,128)(2,1)} %copy-done.1, ...), kind=kOutput, calls=%fused_computation.3 | convolution fusion | flops 1676738560 | bytes 47251972 | tf_op jit(solution)/shard_map/dot_general | solution.py:23
  146.3 9.4 %multiply_reduce_fusion = (f32[]{:T(128)}, f32[1792,1792]{1,0:T(8,128)}) fusion(f32[1792,1792]{1,0:T(8,128)} %copy-done, bf16[128,1792]{1,0:T(8,128)(2,1)S(1)} %copy-done.9, bf16[1,1,128,1792]{3,2,1,0:T(8,128)(2,1)S(1)} %copy.25, bf16[1,1,128,1792]{3,2,1,0:T(8,128)(2,1)S(1)} %copy-done.2, f32[128,1792]{1,0:T(8,128)S(1)} %fusion), kind=kOutput, calls=%fused_computation.2 | convolution fusion | flops 838598656 | bytes 27983876 | tf_op jit(solution)/shard_map/dot_general | solution.py:23
  157.0 7.3 %psum.37 = f32[]{:T(128)} all-reduce(f32[]{:T(128)S(6)} %add.98), channel_id=1, replica_groups=mesh['tp'=4,'client'=4,'region'=2] {'tp'}, use_global_device_ids=true, to_apply=%region_6.0 | all-reduce | flops 1 | bytes 8 | tf_op jit(solution)/shard_map/psum | solution.py:64
  165.0 8.3 %multiply_convert_fusion = bf16[1792,1792]{1,0:T(8,128)(2,1)} fusion(f32[1792,1792]{1,0:T(8,128)} %get-tuple-element.15, f32[]{:T(128)S(6)} %mul.214), kind=kLoop, calls=%fused_computation | loop fusion | flops 6422528 | bytes 19267588 | tf_op jit(solution)/shard_map/convert_element_type | solution.py:68
  173.3 9.7 %copy.20 = bf16[1792,1792]{0,1:T(8,128)(2,1)} copy(bf16[1792,1792]{1,0:T(8,128)(2,1)} %multiply_convert_fusion) | data formatting | bytes 12845056
  183.0 0.0 reduce-scatter.7.cloned.1.call-update
  183.0 0.0 reduce-scatter.5.cloned.1.call-start
  183.1 9.0 %multiply_convert_fusion.1 = bf16[1792,1792]{1,0:T(8,128)(2,1)} fusion(f32[1792,1792]{1,0:T(8,128)} %get-tuple-element.13, f32[]{:T(128)S(6)} %mul.214), kind=kLoop, calls=%fused_computation.1 | loop fusion | flops 6422528 | bytes 19267588 | tf_op jit(solution)/shard_map/convert_element_type | solution.py:67
  192.1 0.0 reduce-scatter.5.cloned.1.call-update
  192.1 0.0 all-reduce.9.cloned.1.call-start
  192.2 103.6 %reduce-scatter.7.cloned.1.call-done = bf16[448,1792]{1,0:T(8,128)(2,1)} async-done(((bf16[1792,1792]{1,0:T(8,128)(2,1)}), bf16[448,1792]{1,0:T(8,128)(2,1)}) %reduce-scatter.7.cloned.1.call-update) | async-done | bytes 1605648
  295.7 3.7 copy.21
  299.4 111.9 %reduce-scatter.5.cloned.1.call-done = bf16[448,1792]{1,0:T(8,128)(2,1)} async-done(((bf16[1792,1792]{1,0:T(8,128)(2,1)}), bf16[448,1792]{1,0:T(8,128)(2,1)}) %reduce-scatter.5.cloned.1.call-update) | async-done | bytes 1605648 | tf_op jit(solution)/shard_map/reduce_scatter | solution.py:72
  411.3 0.0 all-reduce.9.cloned.1.call-update
  411.4 1.9 copy.18
  413.3 93.8 %all-reduce.9.cloned.1.call-done = (bf16[448,1792]{1,0:T(8,128)(2,1)}, bf16[1792,448]{1,0:T(8,128)(2,1)}) async-done(((bf16[448,1792]{1,0:T(8,128)(2,1)}, bf16[1792,448]{1,0:T(8,128)(2,1)}), (bf16[448,1792]{1,0:T(8,128)(2,1)}, bf16[1792,448]{1,0:T(8,128)(2,1)})) %all-reduce.9.cloned.1.call-update) | async-done | bytes 3211280 | tf_op jit(solution)/shard_map/psum | solution.py:85
  507.0 3.7 multiply_add_fusion
  510.8 2.7 copy.19
  513.5 2.8 multiply_add_fusion.1
  (34 shorter events, 0.1 us)
Async XLA Ops:
  7.2 55.8 %all-reduce.5.cloned.1.call-start = ((), (), s32[]{:S(2)}) async-start(), calls=%async_computation.2 | async-start | bytes 917504 | tf_op jit(solution)/shard_map/psum | solution.py:47
  18.2 9.7 %slice-start = ((s8[6422528]{0:T(1024)(128)(4,1)}), s8[2228224]{0:T(1024)(128)(4,1)S(1)}, s32[]{:S(2)}) async-start(s8[6422528]{0:T(1024)(128)(4,1)} %bitcast.59), calls=%async_computation.7 | async-start | bytes 4456448
  22.8 40.2 %copy-start.3 = (bf16[1,1,128,1792]{3,2,1,0:T(8,128)(2,1)}, bf16[1,1,128,1792]{3,2,1,0:T(8,128)(2,1)S(1)}, u32[]{:S(2)}) copy-start(bf16[1,1,128,1792]{3,2,1,0:T(8,128)(2,1)S(1)} %copy.22) | copy-start | bytes 1376260
  23.0 5.0 slice-start.1
  23.0 7.0 %copy-start.12 = (bf16[1,2,128,448]{2,3,1,0:T(8,128)(2,1)S(1)}, bf16[1,2,128,448]{2,3,1,0:T(8,128)(2,1)}, u32[]{:S(2)}) copy-start(bf16[1,2,128,448]{2,3,1,0:T(8,128)(2,1)} %param.7) | copy-start | bytes 688132
  27.0 0.9 copy-start.5
  29.9 97.0 %all-reduce.7.cloned.1.call-start = ((), (), s32[]{:S(2)}) async-start(), calls=%async_computation.3 | async-start | bytes 917504 | tf_op jit(solution)/shard_map/psum | solution.py:47
  45.5 1.2 copy-start.1
  46.6 16.4 %copy-start.7 = (bf16[1,1,128,1792]{3,2,1,0:T(8,128)(2,1)}, bf16[1,1,128,1792]{3,2,1,0:T(8,128)(2,1)S(1)}, u32[]{:S(2)}) copy-start(bf16[1,1,128,1792]{3,2,1,0:T(8,128)(2,1)S(1)} %copy.23) | copy-start | bytes 1376260
  63.0 27.4 %slice-start.2 = ((s8[6422528]{0:T(1024)(128)(4,1)}), s8[2228224]{0:T(1024)(128)(4,1)S(1)}, s32[]{:S(2)}) async-start(s8[6422528]{0:T(1024)(128)(4,1)} %bitcast.61), calls=%async_computation.9 | async-start | bytes 4456448
  74.8 8.8 %copy-start.4 = (bf16[1,1,128,1792]{3,2,1,0:T(8,128)(2,1)S(1)}, bf16[1,1,128,1792]{3,2,1,0:T(8,128)(2,1)}, u32[]{:S(2)}) copy-start(bf16[1,1,128,1792]{3,2,1,0:T(8,128)(2,1)} %copy-done.3) | copy-start | bytes 1376260
  74.8 8.9 %copy-start.6 = (f32[128,1792]{1,0:T(8,128)S(1)}, f32[128,1792]{1,0:T(8,128)}, u32[]{:S(2)}) copy-start(f32[128,1792]{1,0:T(8,128)} %copy-done.5) | copy-start | bytes 2752516
  74.8 8.9 %copy-start.8 = (bf16[1,1,128,1792]{3,2,1,0:T(8,128)(2,1)S(1)}, bf16[1,1,128,1792]{3,2,1,0:T(8,128)(2,1)}, u32[]{:S(2)}) copy-start(bf16[1,1,128,1792]{3,2,1,0:T(8,128)(2,1)} %copy-done.7) | copy-start | bytes 1376260
  74.8 8.9 %copy-start.10 = (bf16[128,1792]{1,0:T(8,128)(2,1)S(1)}, bf16[128,1792]{1,0:T(8,128)(2,1)}, u32[]{:S(2)}) copy-start(bf16[128,1792]{1,0:T(8,128)(2,1)} %all-reduce.5.cloned.1.call-done) | copy-start | bytes 1376260
  74.8 15.6 %slice-start.3 = ((s8[6422528]{0:T(1024)(128)(4,1)}), s8[4194304]{0:T(1024)(128)(4,1)S(1)}, s32[]{:S(2)}) async-start(s8[6422528]{0:T(1024)(128)(4,1)} %bitcast.61), calls=%async_computation.10 | async-start | bytes 8388608
  85.7 4.6 copy-start
  93.6 202.1 %reduce-scatter.7.cloned.1.call-start = ((), (), s32[]{:S(2)}) async-start(), calls=%async_computation.5 | async-start | bytes 8028160
  96.3 50.0 %copy-start.2 = (bf16[1,1,128,1792]{3,2,1,0:T(8,128)(2,1)S(1)}, bf16[1,1,128,1792]{3,2,1,0:T(8,128)(2,1)}, u32[]{:S(2)}) copy-start(bf16[1,1,128,1792]{3,2,1,0:T(8,128)(2,1)} %copy-done.1) | copy-start | bytes 1376260
  126.9 19.4 %copy-start.9 = (bf16[128,1792]{1,0:T(8,128)(2,1)S(1)}, bf16[128,1792]{1,0:T(8,128)(2,1)}, u32[]{:S(2)}) copy-start(bf16[128,1792]{1,0:T(8,128)(2,1)} %all-reduce.7.cloned.1.call-done) | copy-start | bytes 1376260
  183.0 228.3 %reduce-scatter.5.cloned.1.call-start = ((), (), s32[]{:S(2)}) async-start(), calls=%async_computation.4 | async-start | bytes 8028160 | tf_op jit(solution)/shard_map/reduce_scatter | solution.py:72
  192.1 314.9 %all-reduce.9.cloned.1.call-start = ((), (), s32[]{:S(2)}) async-start(), calls=%async_computation.6 | async-start | bytes 6881280 | tf_op jit(solution)/shard_map/psum | solution.py:85
  411.4 102.1 %copy-start.11 = (f32[224,1792]{1,0:T(8,128)S(1)}, f32[224,1792]{1,0:T(8,128)}, u32[]{:S(2)}) copy-start(f32[224,1792]{1,0:T(8,128)} %param.10) | copy-start | bytes 4816900
Sparse Core Ops, SparseCore 0:
  30.0 32.8 all-reduce.4
  93.8 33.0 all-reduce.6
  183.2 112.5 reduce-scatter.6
  297.9 113.3 reduce-scatter.4
  413.6 93.4 all-reduce.8
where the time goes:
time: 525 us; the launch traced here: 523 us
  waiting for transfers between devices  356 us (68%)
  matrix products  60.7 us (12%)
  local copies, waits for them, and re-layouts  37.3 us (7%)
  blocking collectives  28 us (5%)
  other arithmetic  24.2 us (5%)
  between operations  16 us (3%)
    reduce_scatter x1, waiting for transfers between devices, shards(): lax.psum_scatter(clip_up.astype(jnp.bfloat16), 'client', scatter_dimensio...  112 us
    unnamed x6, waiting for transfers between devices  104 us
    psum x1, waiting for transfers between devices, shards(): lax.psum(summed_up.astype(jnp.bfloat16), 'region').astype(jnp.float32)  93.8 us
    psum x2, waiting for transfers between devices, shards(): lax.psum(partial_out.astype(jnp.bfloat16), 'tp').astype(jnp.float32)  46.9 us
    dot_general x4, matrix products, contract_rows(): lax.dot_general(left, right, (((0,), (0,)), ((), ())), preferred_element_...  42.7 us
    unnamed x44, local copies, waits for them, and re-layouts  33 us
    dot_general x2, matrix products, shards(): pre = jnp.dot(normed, w_up, preferred_element_type=jnp.float32)  12.8 us
    all_gather x1, blocking collectives, shards(): lax.all_gather(target, 'tp', axis=3, tiled=True)  10.8 us
  transfers between devices with their start and end apart: 5, of which 5 were waited for; matrix products, arithmetic and copies ran while one was open for 4% of the time, Pallas kernels for 0%

commit v1 on v0

--- a/solution.py
+++ b/solution.py
@@ -97,7 +97,117 @@
     return (new_up, new_down)
 
 
+def dot(left, right):
+    return jnp.dot(left, right, preferred_element_type=jnp.float32)
+
+
+def dot_t(left, right):
+    return lax.dot_general(
+        left,
+        right,
+        (((left.ndim - 1,), (right.ndim - 1,)), (tuple(range(left.ndim - 2)),) * 2),
+        preferred_element_type=jnp.float32,
+    )
+
+
+def gelu(pre):
+    return jax.nn.gelu(pre, approximate=True).astype(jnp.bfloat16)
+
+
+def normalise(inputs):
+    xfloat = inputs.astype(jnp.float32)
+    return (
+        xfloat * lax.rsqrt(jnp.mean(xfloat * xfloat, axis=-1, keepdims=True) + 1e-06)
+    ).astype(jnp.bfloat16)
+
+
+def recomputed(hidden_in, target, up_weight, down_weight, noise_up, noise_down):
+    both = lax.all_gather(
+        jnp.concatenate([hidden_in, target], 0), "tp", axis=3, tiled=True
+    )
+    inputs, goals = both[0], both[1]
+    tokens = inputs.shape[1]
+    clients = ("client", "region")
+    every = lax.all_gather(inputs, clients)
+    normed = normalise(inputs)
+
+    def residual(partial_out, turn):
+        output = inputs[turn].astype(jnp.float32) + lax.psum(
+            partial_out.astype(jnp.bfloat16), "tp"
+        ).astype(jnp.float32)
+        return ((output - goals[turn].astype(jnp.float32)) / tokens).astype(jnp.bfloat16)
+
+    pre0 = dot(normed[0], up_weight)
+    act0 = gelu(pre0)
+    resid0 = residual(dot(act0, down_weight), 0)
+    every_resid0 = lax.all_gather(resid0, clients)
+    dpre0 = gelu_back(pre0, dot_t(resid0, down_weight)).astype(jnp.bfloat16)
+    overlap = (local_rate * dot_t(normed[1], normed[0])).astype(jnp.bfloat16)
+    act1 = gelu(dot(normed[1], up_weight) - dot(overlap, dpre0))
+    overlap = (local_rate * dot_t(act1, act0)).astype(jnp.bfloat16)
+    resid1 = residual(dot(act1, down_weight) - dot(overlap, resid0), 1)
+    every_resid1 = lax.all_gather(resid1, clients)
+
+    count = every.shape[0]
+    every_normed = normalise(every)
+    first, second = every_normed[:, 0], every_normed[:, 1]
+    pre0 = dot(first, up_weight)
+    act0 = gelu(pre0)
+    dpre0 = gelu_back(pre0, dot_t_flat(every_resid0, down_weight)).astype(jnp.bfloat16)
+    overlap = (local_rate * dot_t(second, first)).astype(jnp.bfloat16)
+    pre1 = dot(second, up_weight) - batched(overlap, dpre0)
+    act1 = gelu(pre1)
+    overlap = (local_rate * dot_t(every_resid1, every_resid0)).astype(jnp.bfloat16)
+    back1 = dot_t_flat(every_resid1, down_weight) - batched(overlap, act0)
+    dpre1 = gelu_back(pre1, back1).astype(jnp.bfloat16)
+
+    rows_n = every_normed.reshape(count, STEPS * tokens, -1)
+    rows_r = jnp.concatenate([every_resid0, every_resid1], 1)
+    rows_a = jnp.concatenate([act0, act1], 1)
+    rows_p = jnp.concatenate([dpre0, dpre1], 1)
+    squared = jnp.sum(
+        dot_t(rows_n, rows_n) * dot_t(rows_p, rows_p)
+        + dot_t(rows_a, rows_a) * dot_t(rows_r, rows_r),
+        axis=(1, 2),
+    )
+    size = local_rate * jnp.sqrt(jnp.maximum(lax.psum(squared, "tp"), 0.0))
+    bound = clip_rms * math.sqrt(2.0 * D * F)
+    factor = (-local_rate * bound / jnp.maximum(size, bound))[:, None, None]
+
+    share = D // count
+    block = lax.axis_index("client") * lax.axis_size("region") + lax.axis_index("region")
+
+    def own(rows):
+        part = lax.dynamic_slice_in_dim(rows, block * share, share, 2)
+        return (part.astype(jnp.float32) * factor).astype(jnp.bfloat16).reshape(-1, share)
+
+    total_up = contract_rows(own(rows_n), rows_p.reshape(count * STEPS * tokens, -1))
+    total_down = contract_rows(rows_a.reshape(count * STEPS * tokens, -1), own(rows_r))
+    base_up = lax.dynamic_slice_in_dim(up_weight, block * share, share, 0).astype(jnp.float32)
+    base_down = lax.dynamic_slice_in_dim(down_weight, block * share, share, 1).astype(jnp.float32)
+    root = math.sqrt(count)
+    scale = server_rate / (clip_rms * root)
+    return (
+        base_up + scale * (total_up + clip_rms * root * noise_up),
+        base_down + scale * (total_down + clip_rms * root * noise_down),
+    )
+
+
+def dot_t_flat(left, right):
+    return lax.dot_general(
+        left, right, (((left.ndim - 1,), (1,)), ((), ())), preferred_element_type=jnp.float32
+    )
+
+
+def batched(left, right):
+    return lax.dot_general(
+        left, right, (((2,), (1,)), ((0,), (0,))), preferred_element_type=jnp.float32
+    )
+
+
 def solution(mesh):
+    few = mesh.shape["client"] * mesh.shape["region"] <= 8
+    body = recomputed if few else shards
     placed = (
         P(("client", "region"), None, None, "tp"),
         P(("client", "region"), None, None, "tp"),
@@ -107,7 +217,7 @@
         P("tp", ("client", "region")),
     )
     return jax.shard_map(
-        shards,
+        body,
         mesh=mesh,
         in_specs=placed,
         out_specs=(P(("client", "region"), "tp"), P("tp", ("client", "region"))),

time: 525 us -> 570 us (1.086)
  the two profiles are of different devices: /device:TPU:25 before, /device:TPU:0 now
where the time goes in v1:
time: 570 us; the launch traced here: 560 us
  waiting for transfers between devices  299 us (52%)
  matrix products  156 us (27%)
  local copies, waits for them, and re-layouts  68.7 us (12%)
  between operations  14.5 us (3%)
  other arithmetic  14 us (2%)
  blocking collectives  6.38 us (1%)
    all_gather x1, waiting for transfers between devices, recomputed(): every = lax.all_gather(inputs, clients)  99.2 us
    all_gather x1, waiting for transfers between devices, recomputed(): every_resid0 = lax.all_gather(resid0, clients)  64.6 us
    all_gather x1, waiting for transfers between devices, recomputed(): every_resid1 = lax.all_gather(resid1, clients)  61.9 us
    dot_general x8, matrix products, dot(): return jnp.dot(left, right, preferred_element_type=jnp.float32)  52.4 us
    psum x2, waiting for transfers between devices, residual(): lax.psum(partial_out.astype(jnp.bfloat16), 'tp').astype(jnp.float32)  48.8 us
    dot_general x2, matrix products, dot_t_flat(): lax.dot_general(left, right, (((left.ndim - 1,), (1,)), ((), ())), prefer...  35.3 us
    dot_general x4, matrix products, dot_t(): lax.dot_general(left, right, (((left.ndim - 1,), (right.ndim - 1,)), (tup...  34.5 us
    all_gather x1, waiting for transfers between devices, recomputed(): lax.all_gather(jnp.concatenate([hidden_in, target], 0), 'tp', axis=3, til...  23.9 us
  transfers between devices with their start and end apart: 6, of which 6 were waited for; matrix products, arithmetic and copies ran while one was open for 7% of the time, Pallas kernels for 0%

profile of v1, /device:TPU:0, one launch (start us, length us, event | category | flops | bytes accessed | tf_op | source)
XLA Modules:
  0.0 559.9 jit_solution(13832750058235620481)
XLA Ops:
  7.2 1.2 copy.55
  8.4 1.2 copy.56
  9.6 1.4 pad_maximum_fusion.24
  11.1 23.9 %all-gather.7.cloned.1.call-done = bf16[2,2,128,1792]{2,1,0,3:T(2,128)(2,1)} async-done(((bf16[2,2,128,448]{2,1,0,3:T(2,128)(2,1)}), bf16[2,2,128,1792]{2,1,0,3:T(2,128)(2,1)}) %all-gather.7.cloned.1.call-update) | async-done | bytes 1835024 | tf_op jit(solution)/shard_map/all_gather | solution.py:125
  35.0 2.4 slice.47
  37.4 2.5 copy.75
  40.5 0.9 copy-done.7
  41.4 4.0 fusion.82
  45.4 0.9 copy-done.5
  46.4 1.9 convolution_convert_fusion
  48.4 5.4 fusion.104
  53.8 2.3 copy.76
  56.1 2.0 copy.77
  58.1 5.0 fusion.83
  63.1 18.3 %all-reduce.3.cloned.1.call-done = bf16[128,1792]{1,0:T(8,128)(2,1)} async-done(((bf16[128,1792]{1,0:T(8,128)(2,1)}), bf16[128,1792]{1,0:T(8,128)(2,1)}) %all-reduce.3.cloned.1.call-update) | async-done | bytes 458768 | tf_op jit(solution)/shard_map/psum | solution.py:135
  81.4 1.2 fusion.70
  82.6 6.1 %fusion.66 = bf16[128,1792]{1,0:T(8,128)(2,1)S(1)} fusion(f32[128,1792]{1,0:T(8,128)} %fusion.83, f32[128,1792]{1,0:T(8,128)} %copy-done.5, bf16[2,128,1792]{2,1,0:T(8,128)(2,1)} %copy-done.7, bf16[128,1792]{1,0:T(8,128)(2,1)S(1)} %fusion.70, bf16[1792,1792]{1,0:T(8,128)(2,1)} %param.9), kind=kOutput, calls=%fused_computation.92 | convolution fusion | flops 946438144 | bytes 10092544 | tf_op jit(solution)/shard_map/dot_general | solution.py:101
  88.8 4.8 fusion.107
  93.5 3.0 fusion.42
  97.4 1.0 copy.78
  98.4 1.0 copy.79
  99.3 30.5 %all-reduce.5.cloned.1.call-done = bf16[128,1792]{1,0:T(8,128)(2,1)} async-done(((bf16[128,1792]{1,0:T(8,128)(2,1)}), bf16[128,1792]{1,0:T(8,128)(2,1)}) %all-reduce.5.cloned.1.call-update) | async-done | bytes 458768 | tf_op jit(solution)/shard_map/psum | solution.py:135
  129.8 2.0 fusion.68
  132.4 1.7 constant_dynamic-slice_fusion
  134.1 64.6 %all-gather.11.cloned.1.call-done = bf16[1024,1792]{1,0:T(8,128)(2,1)} async-done(((bf16[128,1792]{1,0:T(8,128)(2,1)}), bf16[1024,1792]{1,0:T(8,128)(2,1)}) %all-gather.11.cloned.1.call-update) | async-done | bytes 3670032 | tf_op jit(solution)/shard_map/all_gather | solution.py:143
  198.7 6.0 %copy.66 = bf16[8,128,1792]{1,2,0:T(8,128)(2,1)} copy(bf16[8,128,1792]{2,1,0:T(8,128)(2,1)} %bitcast.107) | data formatting | bytes 7340032 | tf_op jit(solution)/shard_map/all_gather | solution.py:143
  204.7 61.9 %all-gather.13.cloned.1.call-done = bf16[1024,1792]{1,0:T(8,128)(2,1)} async-done(((bf16[128,1792]{1,0:T(8,128)(2,1)}), bf16[1024,1792]{1,0:T(8,128)(2,1)}) %all-gather.13.cloned.1.call-update) | async-done | bytes 3670032 | tf_op jit(solution)/shard_map/all_gather | solution.py:149
  266.6 6.0 %copy.67 = bf16[8,128,1792]{1,2,0:T(8,128)(2,1)} copy(bf16[8,128,1792]{2,1,0:T(8,128)(2,1)} %bitcast.110) | data formatting | bytes 7340032 | tf_op jit(solution)/shard_map/all_gather | solution.py:149
  272.6 7.9 %fusion.2 = f32[8,256,256]{2,1,0:T(8,128)S(1)} fusion(bf16[8,128,1792]{1,2,0:T(8,128)(2,1)} %copy.67, bf16[8,128,1792]{1,2,0:T(8,128)(2,1)} %copy.66), kind=kOutput, calls=%fused_computation.11 | convolution fusion | flops 1893728256 | bytes 9437184 | tf_op jit(solution)/shard_map/dot_general | solution.py:105
  280.5 99.2 %all-gather.9.cloned.1.call-done = bf16[8,2,128,1792]{3,2,1,0:T(8,128)(2,1)} async-done(((bf16[1,2,128,1792]{3,2,1,0:T(8,128)(2,1)}), bf16[8,2,128,1792]{3,2,1,0:T(8,128)(2,1)}) %all-gather.9.cloned.1.call-update) | async-done | bytes 7340048 | tf_op jit(solution)/shard_map/all_gather | solution.py:131
  379.7 4.6 fusion
  384.3 4.3 fusion.1
  388.6 15.9 %multiply_convert_fusion.1 = (bf16[8,128,1792]{2,1,0:T(8,128)(2,1)}, f32[8,128,1792]{2,1,0:T(8,128)}) fusion(bf16[1792,1792]{1,0:T(8,128)(2,1)} %param.8, bf16[8,2,128,1792]{3,2,0,1:T(8,128)(2,1)S(1)} %fusion.1), kind=kOutput, calls=%fused_computation.29 | convolution fusion | flops 6593183744 | bytes 21102592 | tf_op jit(solution)/shard_map/dot_general | solution.py:101
  404.5 11.6 %fusion.17 = f32[8,128,1792]{2,1,0:T(8,128)} fusion(bf16[1792,1792]{1,0:T(8,128)(2,1)} %param.8, bf16[8,2,128,1792]{3,2,0,1:T(8,128)(2,1)S(1)} %fusion.1), kind=kOutput, calls=%fused_computation.30 | convolution fusion | flops 6576668672 | bytes 17432576 | tf_op jit(solution)/shard_map/dot_general | solution.py:101
  416.2 19.1 %copy.59 = bf16[8,2,128,1792]{2,1,3,0:T(2,128)(2,1)} copy(bf16[8,2,128,1792]{3,2,0,1:T(8,128)(2,1)} %copy-done) | data formatting | bytes 14680064 | tf_op jit(solution)/shard_map/convert_element_type | solution.py:121
  435.3 9.2 %fusion.48 = f32[8,128,1792]{2,1,0:T(8,128)} fusion(bf16[8,128,1792]{2,1,0:T(8,128)(2,1)} %get-tuple-element.6, bf16[8,128,1792]{2,1,0:T(8,128)(2,1)} %bitcast.111, bf16[8,128,1792]{2,1,0:T(8,128)(2,1)} %bitcast.108), kind=kOutput, calls=%fused_computation.72 | convolution fusion | flops 939786240 | bytes 18350080 | tf_op jit(solution)/shard_map/dot_general | solution.py:203
  444.5 16.1 %fusion.9 = bf16[8,128,1792]{2,1,0:T(8,128)(2,1)} fusion(f32[8,128,1792]{2,1,0:T(8,128)} %get-tuple-element.7, bf16[8,128,1792]{2,1,0:T(8,128)(2,1)} %bitcast.109, bf16[1792,1792]{1,0:T(8,128)(2,1)} %param.9), kind=kOutput, calls=%fused_computation.18 | convolution fusion | flops 6613368832 | bytes 21102592 | tf_op jit(solution)/shard_map/dot_general | solution.py:197
  460.6 14.4 %multiply_convert_fusion = (bf16[8,128,1792]{2,1,0:T(8,128)(2,1)}, f32[8,128,1792]{2,1,0:T(8,128)}) fusion(f32[8,128,1792]{2,1,0:T(8,128)} %fusion.17, bf16[8,128,1792]{2,1,0:T(8,128)(2,1)} %fusion.9, bf16[8,2,128,1792]{3,2,0,1:T(8,128)(2,1)} %copy-done), kind=kOutput, calls=%fused_computation.28 | convolution fusion | flops 958136320 | bytes 29360128 | tf_op jit(solution)/shard_map/dot_general | solution.py:203
  475.0 19.2 %fusion.16 = bf16[8,128,1792]{2,1,0:T(8,128)(2,1)} fusion(f32[8,128,1792]{2,1,0:T(8,128)} %get-tuple-element.9, f32[8,128,1792]{2,1,0:T(8,128)} %fusion.48, bf16[8,128,1792]{2,1,0:T(8,128)(2,1)} %bitcast.112, bf16[1792,1792]{1,0:T(8,128)(2,1)} %param.9), kind=kOutput, calls=%fused_computation.25 | convolution fusion | flops 6615203840 | bytes 28442624 | tf_op jit(solution)/shard_map/dot_general | solution.py:197
  494.2 8.7 %fusion.30 = f32[8,256,256]{2,1,0:T(8,128)} fusion(bf16[8,128,1792]{2,1,0:T(8,128)(2,1)} %fusion.16, bf16[8,128,1792]{2,1,0:T(8,128)(2,1)} %fusion.9), kind=kOutput, calls=%fused_computation.41 | convolution fusion | flops 1893728256 | bytes 9437184 | tf_op jit(solution)/shard_map/dot_general | solution.py:105
  502.9 8.9 %fusion.28 = f32[8,256,256]{2,1,0:T(8,128)} fusion(bf16[8,128,1792]{2,1,0:T(8,128)(2,1)} %get-tuple-element.8, bf16[8,128,1792]{2,1,0:T(8,128)(2,1)} %get-tuple-element.6), kind=kOutput, calls=%fused_computation.39 | convolution fusion | flops 1893728256 | bytes 9437184 | tf_op jit(solution)/shard_map/dot_general | solution.py:105
  511.9 12.4 %reshape.46 = bf16[8,256,1792]{1,2,0:T(8,128)(2,1)} reshape(bf16[8,2,128,1792]{2,1,3,0:T(2,128)(2,1)} %copy.59) | data formatting | bytes 14680064 | tf_op jit(solution)/shard_map/reshape | solution.py:164
  524.3 8.9 %add_reduce_fusion = f32[8]{0:T(128)S(1)} fusion(f32[8,256,256]{2,1,0:T(8,128)} %fusion.28, f32[8,256,256]{2,1,0:T(8,128)S(1)} %fusion.2, f32[8,256,256]{2,1,0:T(8,128)} %fusion.30, bf16[8,256,1792]{1,2,0:T(8,128)(2,1)} %reshape.46), kind=kOutput, calls=%fused_computation.60 | convolution fusion | flops 1881145344 | bytes 13631520 | tf_op jit(solution)/shard_map/dot_general | solution.py:105
  533.8 6.4 %psum.23 = f32[8]{0:T(128)S(1)} all-reduce(f32[8]{0:T(128)S(1)} %add_reduce_fusion), channel_id=1, replica_groups=mesh['tp'=4,'client'=4,'region'=2] {'tp'}, use_global_device_ids=true, to_apply=%region_5.0 | all-reduce | flops 8 | bytes 64 | tf_op jit(solution)/shard_map/psum | solution.py:173
  540.2 7.3 %fusion.39 = f32[224,1792]{1,0:T(8,128)} fusion(bf16[8,128,1792]{2,1,0:T(8,128)(2,1)} %fusion.16, bf16[8,128,1792]{2,1,0:T(8,128)(2,1)} %fusion.9, f32[224,1792]{1,0:T(8,128)} %param.10, f32[8]{0:T(128)S(1)} %maximum_divide_fusion, bf16[8,256,1792]{1,2,0:T(8,128)(2,1)} %reshape.46, s32[]{:T(128)S(6)} %select_n.2, bf16[1792,1792]{1,0:T(8,128)(2,1)} %param.8), kind=kOutput, calls=%fused_computation.51 | convolution fusion | flops 1662230528 | bytes 12272672 | tf_op jit(solution)/shard_map/dot_general | solution.py:23
  547.7 0.7 copy-done.9
  548.5 1.1 copy-done.10
  549.6 3.2 fusion.41
  (41 shorter events, 2.9 us)
Async XLA Ops:
  7.2 27.8 %all-gather.7.cloned.1.call-start = ((), (), s32[]{:S(2)}) async-start(), calls=%async_computation | async-start | bytes 2293760 | tf_op jit(solution)/shard_map/all_gather | solution.py:125
  11.0 35.4 %slice-start = ((s8[6422528]{0:T(1024)(128)(4,1)}), s8[2228224]{0:T(1024)(128)(4,1)S(1)}, s32[]{:S(2)}) async-start(s8[6422528]{0:T(1024)(128)(4,1)} %bitcast.105), calls=%async_computation.6 | async-start | bytes 4456448
  11.0 70.4 %all-reduce.3.cloned.1.call-start = ((), (), s32[]{:S(2)}) async-start(), calls=%async_computation.2 | async-start | bytes 917504 | tf_op jit(solution)/shard_map/psum | solution.py:135
  40.0 8.3 %copy-start.1 = (bf16[1,2,128,1792]{3,2,1,0:T(8,128)(2,1)}, bf16[1,2,128,1792]{3,2,1,0:T(8,128)(2,1)S(1)}, u32[]{:S(2)}) copy-start(bf16[1,2,128,1792]{3,2,1,0:T(8,128)(2,1)S(1)} %copy.75) | copy-start | bytes 2752516
  40.5 0.9 copy-start.7
  41.4 4.9 slice-start.1
  45.4 0.9 copy-start.5
  48.3 81.5 %all-reduce.5.cloned.1.call-start = ((), (), s32[]{:S(2)}) async-start(), calls=%async_computation.3 | async-start | bytes 917504 | tf_op jit(solution)/shard_map/psum | solution.py:135
  58.1 23.3 %copy-start.8 = (bf16[1,1,128,1792]{3,2,1,0:T(8,128)(2,1)S(1)}, bf16[1,1,128,1792]{3,2,1,0:T(8,128)(2,1)}, u32[]{:S(2)}) copy-start(bf16[1,1,128,1792]{3,2,1,0:T(8,128)(2,1)} %copy.77) | copy-start | bytes 1376260
  82.6 10.9 %copy-start.2 = (bf16[128,1792]{1,0:T(8,128)(2,1)}, bf16[128,1792]{1,0:T(8,128)(2,1)S(1)}, u32[]{:S(2)}) copy-start(bf16[128,1792]{1,0:T(8,128)(2,1)S(1)} %fusion.70) | copy-start | bytes 1376260
  96.6 102.1 %all-gather.11.cloned.1.call-start = ((), (), s32[]{:S(2)}) async-start(), calls=%async_computation.4 | async-start | bytes 4128768 | tf_op jit(solution)/shard_map/all_gather | solution.py:143
  97.1 169.4 %all-gather.13.cloned.1.call-start = ((), (), s32[]{:S(2)}) async-start(), calls=%async_computation.5 | async-start | bytes 4128768 | tf_op jit(solution)/shard_map/all_gather | solution.py:149
  131.8 247.9 %all-gather.9.cloned.1.call-start = ((), (), s32[]{:S(2)}) async-start(), calls=%async_computation.1 | async-start | bytes 8257536 | tf_op jit(solution)/shard_map/all_gather | solution.py:131
  388.6 15.9 %copy-start = (bf16[8,2,128,1792]{3,2,0,1:T(8,128)(2,1)}, bf16[8,2,128,1792]{3,2,0,1:T(8,128)(2,1)S(1)}, u32[]{:S(2)}) copy-start(bf16[8,2,128,1792]{3,2,0,1:T(8,128)(2,1)S(1)} %fusion.1) | copy-start | bytes 22020100
  540.2 7.3 %copy-start.3 = (bf16[8,128,1792]{1,2,0:T(8,128)(2,1)S(1)}, bf16[8,128,1792]{1,2,0:T(8,128)(2,1)}, u32[]{:S(2)}) copy-start(bf16[8,128,1792]{1,2,0:T(8,128)(2,1)} %copy.66) | copy-start | bytes 11010052
  540.2 7.3 %copy-start.4 = (bf16[8,128,1792]{1,2,0:T(8,128)(2,1)S(1)}, bf16[8,128,1792]{1,2,0:T(8,128)(2,1)}, u32[]{:S(2)}) copy-start(bf16[8,128,1792]{1,2,0:T(8,128)(2,1)} %copy.67) | copy-start | bytes 11010052
  540.2 7.6 %copy-start.6 = (bf16[8,128,1792]{2,1,0:T(8,128)(2,1)S(1)}, bf16[8,128,1792]{2,1,0:T(8,128)(2,1)}, u32[]{:S(2)}) copy-start(bf16[8,128,1792]{2,1,0:T(8,128)(2,1)} %get-tuple-element.6) | copy-start | bytes 11010052
  540.2 8.3 %copy-start.9 = (f32[1792,224]{0,1:T(8,128)S(1)}, f32[1792,224]{0,1:T(8,128)}, u32[]{:S(2)}) copy-start(f32[1792,224]{0,1:T(8,128)} %param.11) | copy-start | bytes 4816900
  540.2 9.4 %copy-start.10 = (bf16[8,128,1792]{2,1,0:T(8,128)(2,1)S(1)}, bf16[8,128,1792]{2,1,0:T(8,128)(2,1)}, u32[]{:S(2)}) copy-start(bf16[8,128,1792]{2,1,0:T(8,128)(2,1)} %get-tuple-element.8) | copy-start | bytes 11010052
Sparse Core Ops, SparseCore 0:
  11.1 23.8 all-gather.6
  48.4 32.9 all-reduce.2
  96.7 33.0 all-reduce.4
  131.8 66.8 all-gather.10
  201.3 65.2 all-gather.12
  269.2 110.4 all-gather.8

commit v2 on v0

--- a/solution.py
+++ b/solution.py
@@ -1,8 +1,11 @@
+import functools
 import math
 
 import jax
 import jax.numpy as jnp
 from jax import lax
+from jax.experimental import pallas as pl
+from jax.experimental.pallas import tpu as pltpu
 from jax.sharding import PartitionSpec as P
 
 D = 1792
@@ -97,7 +100,438 @@
     return (new_up, new_down)
 
 
+MESH = pl.DeviceIdType.MESH
+WIDE = 256
+
+
+def dot(left, right):
+    return jnp.dot(left, right, preferred_element_type=jnp.float32)
+
+
+def dot_t(left, right):
+    return lax.dot_general(
+        left, right, (((1,), (1,)), ((), ())), preferred_element_type=jnp.float32
+    )
+
+
+def gelu_pair(pre):
+    root = math.sqrt(2.0 / math.pi)
+    square = pre * pre
+    bent = jnp.tanh(root * (pre + 0.044715 * (square * pre)))
+    half = 0.5 * (1.0 + bent)
+    slope = half + 0.5 * pre * (1.0 - bent * bent) * (root * (1.0 + 0.134145 * square))
+    return pre * half, slope
+
+
+def round_kernel(
+    sizes,
+    hidden,
+    goal,
+    up_hbm,
+    down_hbm,
+    out_up,
+    out_down,
+    up,
+    down,
+    shares,
+    goals,
+    own_x,
+    normed,
+    resid0,
+    resid1,
+    acts,
+    dpres,
+    picked_n,
+    picked_r,
+    later_pre,
+    total,
+    sent,
+    landed,
+    squares,
+    local_sems,
+    in_s,
+    in_r,
+    sum_s,
+    sum_r,
+    z_s,
+    z_r,
+    y_s,
+    y_r,
+    core_s,
+    core_r,
+    tp_s,
+    tp_r,
+):
+    n_tp, n_c, n_r = sizes
+    bf16, f32 = jnp.bfloat16, jnp.float32
+    tp, c, r = lax.axis_index("tp"), lax.axis_index("client"), lax.axis_index("region")
+    tokens, width = own_x.shape[0] // STEPS, own_x.shape[1]
+    local = up.shape[1]
+    blocks = local // WIDE
+    rows = tokens // n_tp
+    part = width // 2
+    core = lax.rem(tp, 2)
+    core_peer = {"tp": tp + 1 - 2 * core}
+    y_peer = {"region": 1 - r}
+    me = c * n_r + r
+    count = n_c * n_r
+
+    def remote(src, dst, send, recv, peer):
+        return pltpu.make_async_remote_copy(
+            src_ref=src, dst_ref=dst, send_sem=send, recv_sem=recv, device_id=peer,
+            device_id_type=MESH,
+        )
+
+    def tp_peer(d):
+        return lax.rem(tp + d, n_tp)
+
+    def tp_from(d):
+        return lax.rem(tp + n_tp - d, n_tp)
+
+    def c_from(d):
+        return lax.rem(c + n_c - d, n_c)
+
+    load_up = pltpu.make_async_copy(up_hbm, up, local_sems.at[0])
+    load_down = pltpu.make_async_copy(down_hbm, down, local_sems.at[1])
+    load_up.start()
+    load_down.start()
+
+    barrier = pltpu.get_barrier_semaphore()
+    for d in range(1, n_tp):
+        pl.semaphore_signal(barrier, inc=1, device_id={"tp": tp_peer(d)}, device_id_type=MESH)
+    for d in range(1, n_c):
+        pl.semaphore_signal(
+            barrier, inc=1, device_id={"client": lax.rem(c + d, n_c)}, device_id_type=MESH
+        )
+    pl.semaphore_signal(barrier, inc=1, device_id=y_peer, device_id_type=MESH)
+    pl.semaphore_wait(barrier, n_tp + n_c - 1)
+
+    pending = []
+
+    def start(copy):
+        copy.start()
+        pending.append(copy)
+        return copy
+
+    for d in range(1, n_tp):
+        start(remote(hidden, shares.at[tp], in_s.at[0, d], in_r.at[0, d], {"tp": tp_peer(d)}))
+    for d in range(1, n_tp):
+        to = pl.multiple_of(tp_peer(d) * rows, rows)
+        start(
+            remote(
+                goal.at[:, pl.ds(to, rows), :], goals.at[tp], in_s.at[1, d], in_r.at[1, d],
+                {"tp": tp_peer(d)},
+            )
+        )
+    shares[tp] = hidden[...]
+    mine = pl.multiple_of(tp * rows, rows)
+    goals[tp] = goal[:, pl.ds(mine, rows), :]
+    for d in range(1, n_tp):
+        slot = shares.at[tp_from(d)]
+        remote(slot, slot, in_s.at[0, d], in_r.at[0, d], {"tp": tp_from(d)}).wait_recv()
+    xfloat = jnp.concatenate([shares[j].astype(f32) for j in range(n_tp)], axis=-1)
+    xfloat = xfloat.reshape(STEPS * tokens, width)
+    own_x[...] = xfloat.astype(bf16)
+    normed[me] = (
+        xfloat * lax.rsqrt(jnp.mean(xfloat * xfloat, axis=-1, keepdims=True) + 1e-06)
+    ).astype(bf16)
+
+    def half(ref, k, which):
+        return ref.at[k, :, pl.ds(pl.multiple_of(which * part, part), part)]
+
+    def z_start(ref, p):
+        for d in range(1, n_c):
+            block = half(ref, me, core)
+            start(
+                remote(
+                    block, block, z_s.at[p, d], z_r.at[p, d], {"client": lax.rem(c + d, n_c)}
+                )
+            )
+        block = half(ref, me, core)
+        start(remote(block, block, y_s.at[p, 0], y_r.at[p, 0], y_peer))
+
+    def z_end(ref, p):
+        for d in range(1, n_c):
+            k = c_from(d) * n_r + r
+            block = half(ref, k, core)
+            remote(
+                block, block, z_s.at[p, d], z_r.at[p, d], {"client": c_from(d)}
+            ).wait_recv()
+            start(remote(block, block, y_s.at[p, d], y_r.at[p, d], y_peer))
+            start(remote(block, block, core_s.at[p, d], core_r.at[p, d], core_peer))
+
+    def y_end(ref, p):
+        for d in range(n_c):
+            k = c_from(d) * n_r + (1 - r)
+            block = half(ref, k, core)
+            remote(block, block, y_s.at[p, d], y_r.at[p, d], y_peer).wait_recv()
+            start(remote(block, block, core_s.at[p, n_c + d], core_r.at[p, n_c + d], core_peer))
+
+    def core_end(ref, p):
+        for d in range(1, 2 * n_c):
+            k = c_from(d % n_c) * n_r + (r if d < n_c else 1 - r)
+            block = half(ref, k, 1 - core)
+            remote(block, block, core_s.at[p, d], core_r.at[p, d], core_peer).wait_recv()
+
+    z_start(normed, 0)
+
+    def columns(b):
+        return pl.ds(pl.multiple_of(b * WIDE, WIDE), WIDE)
+
+    total[...] = jnp.zeros_like(total)
+    load_up.wait()
+    load_down.wait()
+
+    def first(b, unused):
+        at = columns(b)
+        pre = dot(normed[me], up[:, at])
+        later_pre[:, at] = pre[tokens:]
+        act, slope = gelu_pair(pre[:tokens])
+        act = act.astype(bf16)
+        acts[me, :tokens, at] = act
+        dpres[me, :tokens, at] = slope.astype(bf16)
+        total[...] += dot(act, down[at, :])
+        return unused
+
+    lax.fori_loop(0, blocks, first, 0)
+    overlap_n = (local_rate * dot_t(normed[me, tokens:], normed[me, :tokens])).astype(bf16)
+
+    for d in range(1, n_tp):
+        slot = goals.at[tp_from(d)]
+        remote(slot, slot, in_s.at[1, d], in_r.at[1, d], {"tp": tp_from(d)}).wait_recv()
+    goal_rows = jnp.concatenate([goals[j].astype(f32) for j in range(n_tp)], axis=-1)
+
+    def residual(step, ref):
+        sent[step] = total[...].astype(bf16)
+        for d in range(1, n_tp):
+            to = pl.multiple_of(tp_peer(d) * rows, rows)
+            start(
+                remote(
+                    sent.at[step, pl.ds(to, rows), :], landed.at[step, d - 1],
+                    sum_s.at[2 * step, d], sum_r.at[2 * step, d], {"tp": tp_peer(d)},
+                )
+            )
+        output = total[pl.ds(mine, rows), :]
+        for d in range(1, n_tp):
+            slot = landed.at[step, d - 1]
+            remote(
+                slot, slot, sum_s.at[2 * step, d], sum_r.at[2 * step, d], {"tp": tp_from(d)}
+            ).wait_recv()
+            output = output + landed[step, d - 1].astype(f32)
+        held = own_x[pl.ds(pl.multiple_of(step * tokens + tp * rows, rows), rows), :]
+        output = output + held.astype(f32)
+        ref[me, pl.ds(mine, rows), :] = ((output - goal_rows[step]) / tokens).astype(bf16)
+        for d in range(1, n_tp):
+            slot = ref.at[me, pl.ds(mine, rows), :]
+            start(
+                remote(
+                    slot, slot, sum_s.at[2 * step + 1, d], sum_r.at[2 * step + 1, d],
+                    {"tp": tp_peer(d)},
+                )
+            )
+        for d in range(1, n_tp):
+            slot = ref.at[me, pl.ds(pl.multiple_of(tp_from(d) * rows, rows), rows), :]
+            remote(
+                slot, slot, sum_s.at[2 * step + 1, d], sum_r.at[2 * step + 1, d],
+                {"tp": tp_from(d)},
+            ).wait_recv()
+
+    residual(0, resid0)
+    z_start(resid0, 1)
+    z_end(normed, 0)
+
+    total[...] = jnp.zeros_like(total)
+
+    def second(b, overlap_a):
+        at = columns(b)
+        back = dot_t(resid0[me], down[at, :])
+        dpre = (back * dpres[me, :tokens, at].astype(f32)).astype(bf16)
+        dpres[me, :tokens, at] = dpre
+        act, slope = gelu_pair(later_pre[:, at] - dot(overlap_n, dpre))
+        act = act.astype(bf16)
+        acts[me, tokens:, at] = act
+        dpres[me, tokens:, at] = slope.astype(bf16)
+        total[...] += dot(act, down[at, :])
+        return overlap_a + dot_t(act, acts[me, :tokens, at])
+
+    overlap_a = lax.fori_loop(0, blocks, second, jnp.zeros((tokens, tokens), f32))
+    total[...] -= dot((local_rate * overlap_a).astype(bf16), resid0[me])
+    y_end(normed, 0)
+    residual(1, resid1)
+    z_start(resid1, 2)
+    z_end(resid0, 1)
+
+    chosen = (
+        lax.broadcasted_iota(jnp.int32, (WIDE, width), 1)
+        == lax.broadcasted_iota(jnp.int32, (WIDE, width), 0) + me * (width // count)
+    )
+    chosen = jnp.where(chosen, 1.0, 0.0).astype(bf16)
+
+    def last_back(k):
+        overlap_r = (local_rate * dot_t(resid1[k], resid0[k])).astype(bf16)
+
+        def body(b, unused):
+            at = columns(b)
+            back = dot_t(resid1[k], down[at, :]) - dot(overlap_r, acts[k, :tokens, at])
+            dpres[k, tokens:, at] = (back * dpres[k, tokens:, at].astype(f32)).astype(bf16)
+            return unused
+
+        lax.fori_loop(0, blocks, body, 0)
+        picked_r[k, :, :tokens] = dot_t(chosen, resid0[k]).astype(bf16)
+        picked_r[k, :, tokens:] = dot_t(chosen, resid1[k]).astype(bf16)
+
+    last_back(me)
+    picked_n[me] = dot_t(chosen, normed[me]).astype(bf16)
+    rows_r = jnp.concatenate([resid0[me], resid1[me]], axis=0)
+    products = dot_t(normed[me], normed[me]) * dot_t(dpres[me], dpres[me])
+    products = products + dot_t(acts[me], acts[me]) * dot_t(rows_r, rows_r)
+    squares[tp, me] = jnp.broadcast_to(jnp.sum(products, keepdims=True), squares.shape[2:])
+    for d in range(1, n_c):
+        slot = squares.at[tp, me]
+        start(
+            remote(slot, slot, z_s.at[3, d], z_r.at[3, d], {"client": lax.rem(c + d, n_c)})
+        )
+    slot = squares.at[tp, me]
+    start(remote(slot, slot, y_s.at[3, 0], y_r.at[3, 0], y_peer))
+
+    y_end(resid0, 1)
+    z_end(resid1, 2)
+    core_end(normed, 0)
+    core_end(resid0, 1)
+
+    def early(j, unused):
+        k = lax.rem(me + j, count)
+        overlap = (local_rate * dot_t(normed[k, tokens:], normed[k, :tokens])).astype(bf16)
+
+        def body(b, unused):
+            at = columns(b)
+            pre = dot(normed[k], up[:, at])
+            back = dot_t(resid0[k], down[at, :])
+            act, slope = gelu_pair(pre[:tokens])
+            acts[k, :tokens, at] = act.astype(bf16)
+            dpre = (back * slope).astype(bf16)
+            dpres[k, :tokens, at] = dpre
+            act, slope = gelu_pair(pre[tokens:] - dot(overlap, dpre))
+            acts[k, tokens:, at] = act.astype(bf16)
+            dpres[k, tokens:, at] = slope.astype(bf16)
+            return unused
+
+        lax.fori_loop(0, blocks, body, 0)
+        picked_n[k] = dot_t(chosen, normed[k]).astype(bf16)
+        return unused
+
+    lax.fori_loop(1, count // 2, early, 0)
+    y_end(resid1, 2)
+    for d in range(1, n_c):
+        slot = squares.at[tp, c_from(d) * n_r + r]
+        remote(slot, slot, z_s.at[3, d], z_r.at[3, d], {"client": c_from(d)}).wait_recv()
+        start(remote(slot, slot, y_s.at[3, d], y_r.at[3, d], y_peer))
+    lax.fori_loop(count // 2, count, early, 0)
+    for d in range(n_c):
+        slot = squares.at[tp, c_from(d) * n_r + (1 - r)]
+        remote(slot, slot, y_s.at[3, d], y_r.at[3, d], y_peer).wait_recv()
+    for d in range(1, n_tp):
+        slot = squares.at[tp]
+        start(remote(slot, slot, tp_s.at[d], tp_r.at[d], {"tp": tp_peer(d)}))
+    core_end(resid1, 2)
+
+    def late(j, unused):
+        last_back(lax.rem(me + j, count))
+        return unused
+
+    lax.fori_loop(1, count, late, 0)
+    for d in range(1, n_tp):
+        slot = squares.at[tp_from(d)]
+        remote(slot, slot, tp_s.at[d], tp_r.at[d], {"tp": tp_from(d)}).wait_recv()
+
+    out_up[...] = jnp.zeros_like(out_up)
+    out_down[...] = jnp.zeros_like(out_down)
+    bound = clip_rms * math.sqrt(2.0 * width * local * n_tp)
+
+    def add(k, unused):
+        square = squares[0, k]
+        for t in range(1, n_tp):
+            square = square + squares[t, k]
+        size = local_rate * jnp.sqrt(jnp.maximum(square, 0.0))
+        factor = (-local_rate * bound / jnp.maximum(size, bound))[:1]
+        left = (picked_n[k].astype(f32) * factor).astype(bf16)
+        out_up[...] += dot(left, dpres[k])
+        left = (picked_r[k].astype(f32) * factor).astype(bf16)
+        out_down[...] += dot(left, acts[k])
+        return unused
+
+    lax.fori_loop(0, count, add, 0)
+    for copy in pending:
+        copy.wait_send()
+
+
+def gathered(sizes, hidden_in, target, up_weight, down_weight, noise_up, noise_down):
+    n_tp, n_c, n_r = sizes
+    count = n_c * n_r
+    steps, tokens, share = hidden_in.shape[1:]
+    width, local = up_weight.shape
+    both = steps * tokens
+    bf16, f32 = jnp.bfloat16, jnp.float32
+    vmem = pl.BlockSpec(memory_space=pltpu.VMEM)
+    dma = pltpu.SemaphoreType.DMA
+    total_up, total_down = pl.pallas_call(
+        functools.partial(round_kernel, sizes),
+        out_shape=[jax.ShapeDtypeStruct((WIDE, local), f32)] * 2,
+        in_specs=[vmem, vmem] + [pl.BlockSpec(memory_space=pl.ANY)] * 2,
+        out_specs=[vmem, vmem],
+        scratch_shapes=[
+            pltpu.VMEM((width, local), bf16),
+            pltpu.VMEM((local, width), bf16),
+            pltpu.VMEM((n_tp, steps, tokens, share), bf16),
+            pltpu.VMEM((n_tp, steps, tokens // n_tp, share), bf16),
+            pltpu.VMEM((both, width), bf16),
+            pltpu.VMEM((count, both, width), bf16),
+            pltpu.VMEM((count, tokens, width), bf16),
+            pltpu.VMEM((count, tokens, width), bf16),
+            pltpu.VMEM((count, both, local), bf16),
+            pltpu.VMEM((count, both, local), bf16),
+            pltpu.VMEM((count, WIDE, both), bf16),
+            pltpu.VMEM((count, WIDE, both), bf16),
+            pltpu.VMEM((tokens, local), f32),
+            pltpu.VMEM((tokens, width), f32),
+            pltpu.VMEM((steps, tokens, width), bf16),
+            pltpu.VMEM((steps, n_tp - 1, tokens // n_tp, width), bf16),
+            pltpu.VMEM((n_tp, count, 8, both), f32),
+            dma((2,)),
+            dma((2, n_tp)),
+            dma((2, n_tp)),
+            dma((2 * steps, n_tp)),
+            dma((2 * steps, n_tp)),
+            dma((4, n_c)),
+            dma((4, n_c)),
+            dma((4, n_c)),
+            dma((4, n_c)),
+            dma((3, 2 * n_c)),
+            dma((3, 2 * n_c)),
+            dma((n_tp,)),
+            dma((n_tp,)),
+        ],
+        compiler_params=pltpu.CompilerParams(
+            collective_id=0, has_side_effects=True, vmem_limit_bytes=62 * 1024 * 1024
+        ),
+    )(hidden_in[0], target[0], up_weight, down_weight)
+
+    rows = width // count
+    block = lax.axis_index("client") * n_r + lax.axis_index("region")
+    base_up = lax.dynamic_slice_in_dim(up_weight, block * rows, rows, 0).astype(f32)
+    base_down = lax.dynamic_slice_in_dim(down_weight, block * rows, rows, 1).astype(f32)
+    root = math.sqrt(count)
+    scale = server_rate / (clip_rms * root)
+    return (
+        base_up + scale * (total_up[:rows] + clip_rms * root * noise_up),
+        base_down + scale * (total_down[:rows].T + clip_rms * root * noise_down),
+    )
+
+
 def solution(mesh):
+    sizes = tuple(mesh.shape[axis] for axis in ("tp", "client", "region"))
+    few = sizes[1] * sizes[2] <= 8 and sizes[2] == 2 and sizes[0] % 2 == 0
+    body = functools.partial(gathered, sizes) if few else shards
     placed = (
         P(("client", "region"), None, None, "tp"),
         P(("client", "region"), None, None, "tp"),
@@ -107,7 +541,7 @@
         P("tp", ("client", "region")),
     )
     return jax.shard_map(
-        shards,
+        body,
         mesh=mesh,
         in_specs=placed,
         out_specs=(P(("client", "region"), "tp"), P("tp", ("client", "region"))),

time: 525 us -> 212 us (0.40)
  waiting for transfers between devices: 356 us -> 0 us
  Pallas kernels: 0 us -> 199 us
  matrix products: 60.7 us -> 0 us
  local copies, waits for them, and re-layouts: 37.3 us -> 5.95 us
  blocking collectives: 28 us -> 0 us
  other arithmetic: 24.2 us -> 5.9 us
  between operations: 16 us -> 0.67 us
    pallas_call x0 -> x1, Pallas kernels: none -> 199 us  [gathered(): pl.pallas_call(functools.partial(round_kernel, sizes), out_shape=[jax.Sha...]
    psum x3 -> x0, waiting for transfers between devices: 141 us -> none  [the longest x1 93.8 us: shards(): lax.psum(summed_up.astype(jnp.bfloat16), 'region').astype(jnp.float32)]
    reduce_scatter x1 -> x0, waiting for transfers between devices: 112 us -> none  [shards(): lax.psum_scatter(clip_up.astype(jnp.bfloat16), 'client', scatter_dimensio...]
    unnamed x6 -> x0, waiting for transfers between devices: 104 us -> none
    dot_general x8 -> x0, matrix products: 60.7 us -> none  [the longest x4 42.7 us: contract_rows(): lax.dot_general(left, right, (((0,), (0,)), ((), ())), preferred_element_...]
    unnamed x44 -> x7, local copies, waits for them, and re-layouts: 33 us -> 4.12 us
    all_gather x2 -> x0, blocking collectives: 20.7 us -> none  [the longest x1 10.8 us: shards(): lax.all_gather(target, 'tp', axis=3, tiled=True)]
    convert_element_type x2 -> x0, other arithmetic: 17.3 us -> none  [the longest x1 9 us: shards(): (delta_up * factor).astype(jnp.bfloat16)]
  transfers between devices with their start and end apart: 5 -> 0, of which waited for: 5 -> 0; matrix products, arithmetic and copies ran while one was open for 4% -> 0% of each run, Pallas kernels for 0% -> 0%
where the time goes in v2:
time: 212 us; the launch traced here: 211 us
  Pallas kernels  199 us (94%)
  local copies, waits for them, and re-layouts  5.95 us (3%)
  other arithmetic  5.9 us (3%)
    pallas_call x1, Pallas kernels, gathered(): pl.pallas_call(functools.partial(round_kernel, sizes), out_shape=[jax.Sha...  199 us

profile of v2, /device:TPU:25, one launch (start us, length us, event | category | flops | bytes accessed | tf_op | source)
XLA Modules:
  0.0 211.1 jit_solution(17799147259835139919)
XLA Ops:
  0.6 1.8 copy.8
  2.4 1.8 copy.9
  4.2 0.0 copy-start
  4.2 198.5 %shard_map.77 = (f32[256,1792]{1,0:T(8,128)}, f32[256,1792]{1,0:T(8,128)}) custom-call(bf16[2,128,448]{2,1,0:T(8,128)(2,1)} %bitcast.8, bf16[2,128,448]{2,1,0:T(8,128)(2,1)} %bitcast.9, bf16[1792,1792]{1,0:T(8,128)(2,1)} %up_hbm.1, bf16[1792,1792]{1,0:T(8,128)(2,1)} %down_hbm.1), custom_call_target="tpu_custom_call" | custom-call | tf_op jit(solution)/shard_map/pallas_call | solution.py:477
  202.7 0.0 copy-done
  202.8 3.1 %multiply_add_fusion = f32[224,1792]{1,0:T(8,128)} fusion(f32[224,1792]{1,0:T(8,128)S(1)} %copy-done, f32[256,1792]{1,0:T(8,128)} %get-tuple-element.4, bf16[1792,1792]{1,0:T(8,128)(2,1)} %up_hbm.1, s32[]{:T(128)S(6)} %select_n.4), kind=kLoop, calls=%fused_computation.3 | loop fusion | flops 2007040 | bytes 5619716 | tf_op jit(solution)/shard_map/add | solution.py:526
  205.8 0.0 copy-start.1
  205.8 1.8 constant_dynamic-slice_fusion
  207.6 0.6 copy.11
  208.2 0.0 copy-done.1
  208.2 2.8 %fusion.1 = f32[1792,224]{0,1:T(8,128)} fusion(f32[1792,224]{0,1:T(8,128)S(1)} %copy-done.1, f32[256,1792]{1,0:T(8,128)} %get-tuple-element.5, bf16[1792,224]{0,1:T(8,128)(2,1)S(1)} %copy.11), kind=kLoop, calls=%fused_computation.2 | loop fusion | flops 2007040 | bytes 5619712 | tf_op jit(solution)/shard_map/add | solution.py:527
Async XLA Ops:
  4.2 198.6 %copy-start = (f32[224,1792]{1,0:T(8,128)S(1)}, f32[224,1792]{1,0:T(8,128)}, u32[]{:S(2)}) copy-start(f32[224,1792]{1,0:T(8,128)} %param.10) | copy-start | bytes 4816900
  205.8 2.4 %copy-start.1 = (f32[1792,224]{0,1:T(8,128)S(1)}, f32[1792,224]{0,1:T(8,128)}, u32[]{:S(2)}) copy-start(f32[1792,224]{0,1:T(8,128)} %param.11) | copy-start | bytes 4816900

commit v3 on v2

--- a/solution.py
+++ b/solution.py
@@ -169,12 +169,14 @@
     local = up.shape[1]
     blocks = local // WIDE
     rows = tokens // n_tp
+    both = STEPS * tokens
     part = width // 2
     core = lax.rem(tp, 2)
     core_peer = {"tp": tp + 1 - 2 * core}
     y_peer = {"region": 1 - r}
-    me = c * n_r + r
+    me = r * n_c + c
     count = n_c * n_r
+    block = c * n_r + r
 
     def remote(src, dst, send, recv, peer):
         return pltpu.make_async_remote_copy(
@@ -252,7 +254,7 @@
 
     def z_end(ref, p):
         for d in range(1, n_c):
-            k = c_from(d) * n_r + r
+            k = r * n_c + c_from(d)
             block = half(ref, k, core)
             remote(
                 block, block, z_s.at[p, d], z_r.at[p, d], {"client": c_from(d)}
@@ -262,16 +264,22 @@
 
     def y_end(ref, p):
         for d in range(n_c):
-            k = c_from(d) * n_r + (1 - r)
+            k = (1 - r) * n_c + c_from(d)
             block = half(ref, k, core)
             remote(block, block, y_s.at[p, d], y_r.at[p, d], y_peer).wait_recv()
             start(remote(block, block, core_s.at[p, n_c + d], core_r.at[p, n_c + d], core_peer))
 
-    def core_end(ref, p):
-        for d in range(1, 2 * n_c):
-            k = c_from(d % n_c) * n_r + (r if d < n_c else 1 - r)
+    def core_wait(ref, p, sources):
+        for d in sources:
+            k = (r if d < n_c else 1 - r) * n_c + c_from(d % n_c)
             block = half(ref, k, 1 - core)
             remote(block, block, core_s.at[p, d], core_r.at[p, d], core_peer).wait_recv()
+
+    def core_end(ref, p):
+        core_wait(ref, p, range(1, n_c))
+
+    def other_end(ref, p):
+        core_wait(ref, p, range(n_c, 2 * n_c))
 
     z_start(normed, 0)
 
@@ -338,7 +346,6 @@
 
     residual(0, resid0)
     z_start(resid0, 1)
-    z_end(normed, 0)
 
     total[...] = jnp.zeros_like(total)
 
@@ -356,32 +363,25 @@
 
     overlap_a = lax.fori_loop(0, blocks, second, jnp.zeros((tokens, tokens), f32))
     total[...] -= dot((local_rate * overlap_a).astype(bf16), resid0[me])
-    y_end(normed, 0)
+    z_end(normed, 0)
     residual(1, resid1)
     z_start(resid1, 2)
-    z_end(resid0, 1)
 
     chosen = (
         lax.broadcasted_iota(jnp.int32, (WIDE, width), 1)
-        == lax.broadcasted_iota(jnp.int32, (WIDE, width), 0) + me * (width // count)
+        == lax.broadcasted_iota(jnp.int32, (WIDE, width), 0) + block * (width // count)
     )
     chosen = jnp.where(chosen, 1.0, 0.0).astype(bf16)
 
-    def last_back(k):
-        overlap_r = (local_rate * dot_t(resid1[k], resid0[k])).astype(bf16)
-
-        def body(b, unused):
-            at = columns(b)
-            back = dot_t(resid1[k], down[at, :]) - dot(overlap_r, acts[k, :tokens, at])
-            dpres[k, tokens:, at] = (back * dpres[k, tokens:, at].astype(f32)).astype(bf16)
-            return unused
-
-        lax.fori_loop(0, blocks, body, 0)
-        picked_r[k, :, :tokens] = dot_t(chosen, resid0[k]).astype(bf16)
-        picked_r[k, :, tokens:] = dot_t(chosen, resid1[k]).astype(bf16)
-
-    last_back(me)
-    picked_n[me] = dot_t(chosen, normed[me]).astype(bf16)
+    overlap_r = (local_rate * dot_t(resid1[me], resid0[me])).astype(bf16)
+
+    def last(b, unused):
+        at = columns(b)
+        back = dot_t(resid1[me], down[at, :]) - dot(overlap_r, acts[me, :tokens, at])
+        dpres[me, tokens:, at] = (back * dpres[me, tokens:, at].astype(f32)).astype(bf16)
+        return unused
+
+    lax.fori_loop(0, blocks, last, 0)
     rows_r = jnp.concatenate([resid0[me], resid1[me]], axis=0)
     products = dot_t(normed[me], normed[me]) * dot_t(dpres[me], dpres[me])
     products = products + dot_t(acts[me], acts[me]) * dot_t(rows_r, rows_r)
@@ -394,73 +394,119 @@
     slot = squares.at[tp, me]
     start(remote(slot, slot, y_s.at[3, 0], y_r.at[3, 0], y_peer))
 
-    y_end(resid0, 1)
-    z_end(resid1, 2)
+    z_end(resid0, 1)
+    y_end(normed, 0)
     core_end(normed, 0)
     core_end(resid0, 1)
 
-    def early(j, unused):
-        k = lax.rem(me + j, count)
-        overlap = (local_rate * dot_t(normed[k, tokens:], normed[k, :tokens])).astype(bf16)
+    def stacked(ref, at):
+        return ref[at].reshape(n_c * ref.shape[1], ref.shape[2])
+
+    def early(start_slot, low, high):
+        group = pl.ds(start_slot, n_c)
+        overlaps = []
+        for i in range(n_c):
+            k = start_slot + i
+            overlaps.append(
+                (local_rate * dot_t(normed[k, tokens:], normed[k, :tokens])).astype(bf16)
+            )
 
         def body(b, unused):
             at = columns(b)
-            pre = dot(normed[k], up[:, at])
-            back = dot_t(resid0[k], down[at, :])
-            act, slope = gelu_pair(pre[:tokens])
-            acts[k, :tokens, at] = act.astype(bf16)
-            dpre = (back * slope).astype(bf16)
-            dpres[k, :tokens, at] = dpre
-            act, slope = gelu_pair(pre[tokens:] - dot(overlap, dpre))
-            acts[k, tokens:, at] = act.astype(bf16)
-            dpres[k, tokens:, at] = slope.astype(bf16)
+            pre = dot(stacked(normed, group), up[:, at]).reshape(n_c, both, WIDE)
+            back = dot_t(stacked(resid0, group), down[at, :]).reshape(n_c, tokens, WIDE)
+            for i in range(n_c):
+                k = start_slot + i
+                act, slope = gelu_pair(pre[i, :tokens])
+                acts[k, :tokens, at] = act.astype(bf16)
+                dpre = (back[i] * slope).astype(bf16)
+                dpres[k, :tokens, at] = dpre
+                act, slope = gelu_pair(pre[i, tokens:] - dot(overlaps[i], dpre))
+                acts[k, tokens:, at] = act.astype(bf16)
+                dpres[k, tokens:, at] = slope.astype(bf16)
             return unused
 
+        lax.fori_loop(low, high, body, 0)
+
+    def pick(start_slot):
+        group = pl.ds(start_slot, n_c)
+        at = pl.ds(pl.multiple_of(start_slot * both, n_c * both), n_c * both)
+        picked_n[:, at] = dot_t(chosen, stacked(normed, group)).astype(bf16)
+
+    def late(start_slot):
+        group = pl.ds(start_slot, n_c)
+        overlaps = []
+        for i in range(n_c):
+            k = start_slot + i
+            overlaps.append((local_rate * dot_t(resid1[k], resid0[k])).astype(bf16))
+
+        def body(b, unused):
+            at = columns(b)
+            back = dot_t(stacked(resid1, group), down[at, :]).reshape(n_c, tokens, WIDE)
+            for i in range(n_c):
+                k = start_slot + i
+                full = back[i] - dot(overlaps[i], acts[k, :tokens, at])
+                dpres[k, tokens:, at] = (full * dpres[k, tokens:, at].astype(f32)).astype(bf16)
+            return unused
+
         lax.fori_loop(0, blocks, body, 0)
-        picked_n[k] = dot_t(chosen, normed[k]).astype(bf16)
-        return unused
-
-    lax.fori_loop(1, count // 2, early, 0)
-    y_end(resid1, 2)
+        for turn, ref in enumerate((resid0, resid1)):
+            rows_t = dot_t(chosen, stacked(ref, group)).astype(bf16)
+            for i in range(n_c):
+                to = (start_slot + i) * both + turn * tokens
+                picked_r[:, pl.ds(pl.multiple_of(to, tokens), tokens)] = rows_t[
+                    :, i * tokens : (i + 1) * tokens
+                ]
+
+    middle = blocks // 2 + 1
+    early(r * n_c, 0, middle)
+    y_end(resid0, 1)
+    early(r * n_c, middle, blocks)
+    pick(r * n_c)
+    z_end(resid1, 2)
     for d in range(1, n_c):
-        slot = squares.at[tp, c_from(d) * n_r + r]
+        slot = squares.at[tp, r * n_c + c_from(d)]
         remote(slot, slot, z_s.at[3, d], z_r.at[3, d], {"client": c_from(d)}).wait_recv()
         start(remote(slot, slot, y_s.at[3, d], y_r.at[3, d], y_peer))
-    lax.fori_loop(count // 2, count, early, 0)
+    other_end(normed, 0)
+    other_end(resid0, 1)
+    early((1 - r) * n_c, 0, middle)
+    y_end(resid1, 2)
+    early((1 - r) * n_c, middle, blocks)
+    pick((1 - r) * n_c)
     for d in range(n_c):
-        slot = squares.at[tp, c_from(d) * n_r + (1 - r)]
+        slot = squares.at[tp, (1 - r) * n_c + c_from(d)]
         remote(slot, slot, y_s.at[3, d], y_r.at[3, d], y_peer).wait_recv()
     for d in range(1, n_tp):
         slot = squares.at[tp]
         start(remote(slot, slot, tp_s.at[d], tp_r.at[d], {"tp": tp_peer(d)}))
     core_end(resid1, 2)
-
-    def late(j, unused):
-        last_back(lax.rem(me + j, count))
-        return unused
-
-    lax.fori_loop(1, count, late, 0)
+    late(r * n_c)
+    other_end(resid1, 2)
+    late((1 - r) * n_c)
     for d in range(1, n_tp):
         slot = squares.at[tp_from(d)]
         remote(slot, slot, tp_s.at[d], tp_r.at[d], {"tp": tp_from(d)}).wait_recv()
 
-    out_up[...] = jnp.zeros_like(out_up)
-    out_down[...] = jnp.zeros_like(out_down)
     bound = clip_rms * math.sqrt(2.0 * width * local * n_tp)
-
-    def add(k, unused):
-        square = squares[0, k]
+    factors = []
+    for k in range(count):
+        square = squares[0, k, :1]
         for t in range(1, n_tp):
-            square = square + squares[t, k]
+            square = square + squares[t, k, :1]
         size = local_rate * jnp.sqrt(jnp.maximum(square, 0.0))
-        factor = (-local_rate * bound / jnp.maximum(size, bound))[:1]
-        left = (picked_n[k].astype(f32) * factor).astype(bf16)
-        out_up[...] += dot(left, dpres[k])
-        left = (picked_r[k].astype(f32) * factor).astype(bf16)
-        out_down[...] += dot(left, acts[k])
+        factors.append(-local_rate * bound / jnp.maximum(size, bound))
+    factor = jnp.concatenate(factors, axis=-1)
+    picked_n[...] = (picked_n[...].astype(f32) * factor).astype(bf16)
+    picked_r[...] = (picked_r[...].astype(f32) * factor).astype(bf16)
+
+    def add(b, unused):
+        at = columns(b)
+        out_up[:, at] = dot(picked_n[...], dpres[:, :, at].reshape(count * both, WIDE))
+        out_down[:, at] = dot(picked_r[...], acts[:, :, at].reshape(count * both, WIDE))
         return unused
 
-    lax.fori_loop(0, count, add, 0)
+    lax.fori_loop(0, blocks, add, 0)
     for copy in pending:
         copy.wait_send()
 
@@ -490,8 +536,8 @@
             pltpu.VMEM((count, tokens, width), bf16),
             pltpu.VMEM((count, both, local), bf16),
             pltpu.VMEM((count, both, local), bf16),
-            pltpu.VMEM((count, WIDE, both), bf16),
-            pltpu.VMEM((count, WIDE, both), bf16),
+            pltpu.VMEM((WIDE, count * both), bf16),
+            pltpu.VMEM((WIDE, count * both), bf16),
             pltpu.VMEM((tokens, local), f32),
             pltpu.VMEM((tokens, width), f32),
             pltpu.VMEM((steps, tokens, width), bf16),

time: 212 us -> 180 us (0.85)
  Pallas kernels: 199 us -> 167 us
    pallas_call x1, Pallas kernels: 199 us -> 167 us  [gathered(): pl.pallas_call(functools.partial(round_kernel, sizes), out_shape=[jax.Sha...]
where the time goes in v3:
time: 180 us; the launch traced here: 179 us
  Pallas kernels  167 us (93%)
  local copies, waits for them, and re-layouts  5.95 us (3%)
  other arithmetic  5.9 us (3%)
    pallas_call x1, Pallas kernels, gathered(): pl.pallas_call(functools.partial(round_kernel, sizes), out_shape=[jax.Sha...  167 us
    unnamed x7, local copies, waits for them, and re-layouts  4.12 us

profile of v3, /device:TPU:25, one launch (start us, length us, event | category | flops | bytes accessed | tf_op | source)
XLA Modules:
  0.0 179.5 jit_solution(9334197075240652159)
XLA Ops:
  0.6 1.8 copy.8
  2.4 1.8 copy.9
  4.2 0.0 copy-start
  4.2 167.0 %shard_map.77 = (f32[256,1792]{1,0:T(8,128)}, f32[256,1792]{1,0:T(8,128)}) custom-call(bf16[2,128,448]{2,1,0:T(8,128)(2,1)} %bitcast.8, bf16[2,128,448]{2,1,0:T(8,128)(2,1)} %bitcast.9, bf16[1792,1792]{1,0:T(8,128)(2,1)} %up_hbm.1, bf16[1792,1792]{1,0:T(8,128)(2,1)} %down_hbm.1), custom_call_target="tpu_custom_call" | custom-call | tf_op jit(solution)/shard_map/pallas_call | solution.py:523
  171.2 0.0 copy-done
  171.2 3.1 %multiply_add_fusion = f32[224,1792]{1,0:T(8,128)} fusion(f32[224,1792]{1,0:T(8,128)S(1)} %copy-done, f32[256,1792]{1,0:T(8,128)} %get-tuple-element.4, bf16[1792,1792]{1,0:T(8,128)(2,1)} %up_hbm.1, s32[]{:T(128)S(6)} %select_n.4), kind=kLoop, calls=%fused_computation.3 | loop fusion | flops 2007040 | bytes 5619716 | tf_op jit(solution)/shard_map/add | solution.py:572
  174.2 0.0 copy-start.1
  174.2 1.8 %constant_dynamic-slice_fusion = bf16[1792,224]{1,0:T(8,128)(2,1)S(1)} fusion(bf16[1792,1792]{1,0:T(8,128)(2,1)} %down_hbm.1, s32[]{:T(128)S(6)} %select_n.4), kind=kLoop, calls=%fused_computation.4 | loop fusion | bytes 1605636 | tf_op jit(solution)/shard_map/dynamic_slice | solution.py:568
  176.1 0.6 copy.11
  176.6 0.0 copy-done.1
  176.6 2.8 %fusion.1 = f32[1792,224]{0,1:T(8,128)} fusion(f32[1792,224]{0,1:T(8,128)S(1)} %copy-done.1, f32[256,1792]{1,0:T(8,128)} %get-tuple-element.5, bf16[1792,224]{0,1:T(8,128)(2,1)S(1)} %copy.11), kind=kLoop, calls=%fused_computation.2 | loop fusion | flops 2007040 | bytes 5619712 | tf_op jit(solution)/shard_map/add | solution.py:573
Async XLA Ops:
  4.2 167.0 %copy-start = (f32[224,1792]{1,0:T(8,128)S(1)}, f32[224,1792]{1,0:T(8,128)}, u32[]{:S(2)}) copy-start(f32[224,1792]{1,0:T(8,128)} %param.10) | copy-start | bytes 4816900
  174.2 2.4 %copy-start.1 = (f32[1792,224]{0,1:T(8,128)S(1)}, f32[1792,224]{0,1:T(8,128)}, u32[]{:S(2)}) copy-start(f32[1792,224]{0,1:T(8,128)} %param.11) | copy-start | bytes 4816900

commit v4 on v3

--- a/solution.py
+++ b/solution.py
@@ -395,7 +395,6 @@
     start(remote(slot, slot, y_s.at[3, 0], y_r.at[3, 0], y_peer))
 
     z_end(resid0, 1)
-    y_end(normed, 0)
     core_end(normed, 0)
     core_end(resid0, 1)
 
@@ -460,10 +459,11 @@
 
     middle = blocks // 2 + 1
     early(r * n_c, 0, middle)
-    y_end(resid0, 1)
+    y_end(normed, 0)
+    z_end(resid1, 2)
     early(r * n_c, middle, blocks)
     pick(r * n_c)
-    z_end(resid1, 2)
+    y_end(resid0, 1)
     for d in range(1, n_c):
         slot = squares.at[tp, r * n_c + c_from(d)]
         remote(slot, slot, z_s.at[3, d], z_r.at[3, d], {"client": c_from(d)}).wait_recv()
@@ -488,6 +488,7 @@
         slot = squares.at[tp_from(d)]
         remote(slot, slot, tp_s.at[d], tp_r.at[d], {"tp": tp_from(d)}).wait_recv()
 
+    scale = server_rate / (clip_rms * math.sqrt(count))
     bound = clip_rms * math.sqrt(2.0 * width * local * n_tp)
     factors = []
     for k in range(count):
@@ -502,8 +503,10 @@
 
     def add(b, unused):
         at = columns(b)
-        out_up[:, at] = dot(picked_n[...], dpres[:, :, at].reshape(count * both, WIDE))
-        out_down[:, at] = dot(picked_r[...], acts[:, :, at].reshape(count * both, WIDE))
+        summed = dot(picked_n[...], dpres[:, :, at].reshape(count * both, WIDE))
+        out_up[:, at] = scale * summed + dot(chosen, up[:, at])
+        summed = dot(picked_r[...], acts[:, :, at].reshape(count * both, WIDE))
+        out_down[:, at] = scale * summed + dot_t(chosen, down[at, :])
         return unused
 
     lax.fori_loop(0, blocks, add, 0)
@@ -563,14 +566,11 @@
     )(hidden_in[0], target[0], up_weight, down_weight)
 
     rows = width // count
-    block = lax.axis_index("client") * n_r + lax.axis_index("region")
-    base_up = lax.dynamic_slice_in_dim(up_weight, block * rows, rows, 0).astype(f32)
-    base_down = lax.dynamic_slice_in_dim(down_weight, block * rows, rows, 1).astype(f32)
     root = math.sqrt(count)
     scale = server_rate / (clip_rms * root)
     return (
-        base_up + scale * (total_up[:rows] + clip_rms * root * noise_up),
-        base_down + scale * (total_down[:rows].T + clip_rms * root * noise_down),
+        total_up[:rows] + scale * (clip_rms * root * noise_up),
+        total_down[:rows].T + scale * (clip_rms * root * noise_down),
     )
 
 

time: 180 us -> 170 us (0.944)
  Pallas kernels: 167 us -> 161 us
  local copies, waits for them, and re-layouts: 5.95 us -> 3.57 us
    pallas_call x1, Pallas kernels: 167 us -> 161 us  [gathered(): pl.pallas_call(functools.partial(round_kernel, sizes), out_shape=[jax.Sha...]
    dynamic_slice x1 -> x0, local copies, waits for them, and re-layouts: 1.83 us -> none  [gathered(): lax.dynamic_slice_in_dim(down_weight, block * rows, rows, 1).astype(f32)]
    unnamed x7 -> x8, local copies, waits for them, and re-layouts: 4.12 us -> 3.57 us
where the time goes in v4:
time: 170 us; the launch traced here: 169 us
  Pallas kernels  161 us (95%)
  other arithmetic  4.24 us (2%)
  local copies, waits for them, and re-layouts  3.57 us (2%)
    pallas_call x1, Pallas kernels, gathered(): pl.pallas_call(functools.partial(round_kernel, sizes), out_shape=[jax.Sha...  161 us
    unnamed x8, local copies, waits for them, and re-layouts  3.57 us

profile of v4, /device:TPU:25, one launch (start us, length us, event | category | flops | bytes accessed | tf_op | source)
XLA Modules:
  0.0 169.4 jit_solution(17584453552601230779)
XLA Ops:
  0.6 1.8 %copy.8 = bf16[1,2,128,448]{3,2,1,0:T(8,128)(2,1)} copy(bf16[1,2,128,448]{2,3,1,0:T(8,128)(2,1)} %param.6) | data formatting | bytes 458752 | tf_op args[0]
  2.4 1.8 %copy.9 = bf16[1,2,128,448]{3,2,1,0:T(8,128)(2,1)} copy(bf16[1,2,128,448]{2,3,1,0:T(8,128)(2,1)} %param.7) | data formatting | bytes 458752 | tf_op args[1]
  4.2 0.0 copy-start
  4.2 160.9 %shard_map.77 = (f32[256,1792]{1,0:T(8,128)}, f32[256,1792]{1,0:T(8,128)}) custom-call(bf16[2,128,448]{2,1,0:T(8,128)(2,1)} %bitcast.4, bf16[2,128,448]{2,1,0:T(8,128)(2,1)} %bitcast.5, bf16[1792,1792]{1,0:T(8,128)(2,1)} %up_hbm.1, bf16[1792,1792]{1,0:T(8,128)(2,1)} %down_hbm.1), custom_call_target="tpu_custom_call" | custom-call | tf_op jit(solution)/shard_map/pallas_call | solution.py:526
  165.1 0.0 copy-done
  165.1 0.0 copy-start.1
  165.1 0.0 copy-start.2
  165.1 2.9 %multiply_add_fusion = f32[224,1792]{1,0:T(8,128)} fusion(f32[224,1792]{1,0:T(8,128)S(1)} %copy-done, f32[256,1792]{1,0:T(8,128)} %get-tuple-element.4), kind=kLoop, calls=%fused_computation.1 | loop fusion | flops 802816 | bytes 4816896 | tf_op jit(solution)/shard_map/add | solution.py:572
  168.1 0.0 copy-done.1
  168.1 0.0 copy-done.2
  168.1 1.3 bitcast_add_fusion
Async XLA Ops:
  4.2 160.9 %copy-start = (f32[224,1792]{1,0:T(8,128)S(1)}, f32[224,1792]{1,0:T(8,128)}, u32[]{:S(2)}) copy-start(f32[224,1792]{1,0:T(8,128)} %param.10) | copy-start | bytes 4816900
  165.1 2.9 %copy-start.1 = (f32[1792,224]{0,1:T(8,128)S(1)}, f32[1792,224]{0,1:T(8,128)}, u32[]{:S(2)}) copy-start(f32[1792,224]{0,1:T(8,128)} %param.11) | copy-start | bytes 4816900
  165.1 2.9 %copy-start.2 = (f32[256,1792]{1,0:T(8,128)S(1)}, f32[256,1792]{1,0:T(8,128)}, u32[]{:S(2)}) copy-start(f32[256,1792]{1,0:T(8,128)} %get-tuple-element.5) | copy-start | bytes 5505028
